TPU v7x, 256 devices: a whole 4x4x8 slice. The times are simulated.
256 devices in a mesh: size: 4 (over x_hi, core), gz: 64 (over z, y, x_lo).
Axes of the slice: x: 4 (x_hi: 2, x_lo: 2; x = x_hi * 2 + x_lo), y: 4, z: 8, core: 2. Of those that a mesh axis runs over, the one named last changes fastest.
Arguments:
- concentration: float32 [8, 256, 128, 128], P('size', 'gz'), may hold values from 0 to 2
- deposit: float32 [8, 256, 128, 128], P('size', 'gz'), may hold values from 0 to 1
- velocity: float32 [256, 128, 128], P('gz'), may hold values from 0.2 to 1
- pore_label: int32 [256, 128, 128], P('gz'), may hold values from 0 to 3
- diffusivity: float32 [8], P('size'), may hold values from 0.15 to 0.5
- attach_rate: float32 [8], P('size'), may hold values from 0.4 to 4
- volume: float32 [8], P('size'), may hold values from 0.05 to 0.3
- conc_cotangent: float32 [8, 256, 128, 128], P('size', 'gz'), may hold values from -6 to 6
- deposit_cotangent: float32 [8, 256, 128, 128], P('size', 'gz'), may hold values from -6 to 6
Outputs:
- conc_adjoint: float32 [8, 256, 128, 128], P('size', 'gz')
- deposit_adjoint: float32 [8, 256, 128, 128], P('size', 'gz')
All inputs are finite; a program needn't handle non-finite values.
Results may differ from a plain program's by a relative error of at most 0.0001.
Values sent between devices are 32-bit elements; how exact they have to be, the bound alone decides.
No kernel may reach another device: no remote copies, remote signals or barrier semaphores. Data moves between devices by JAX's collectives and lax.ppermute only.
A program may use at most 64 MiB of HBM per device.

v0:
```python
import jax
import jax.numpy as jnp
from jax import lax
from jax.sharding import PartitionSpec as P

CLOGGING = 1.0
TIME_STEP = 0.25
SURFACE_EFF = (0.1, 0.6, 1.2, 2.0)
MIXING = ((0.0, 1.0), (0.75, 0.25), (1.0 / 3.0, 2.0 / 3.0))


def with_halo(array, sides, width):
    for axis, dim in sides:
        peers, length = (lax.axis_size(axis), array.shape[dim])
        up = [(i, (i + 1) % peers) for i in range(peers - 1)]
        down = [(j, i) for i, j in up]
        last = lax.slice_in_dim(array, length - width, length, axis=dim)
        initial = lax.slice_in_dim(array, 0, width, axis=dim)
        before = lax.ppermute(last, axis, up)
        after = lax.ppermute(initial, axis, down)
        array = jnp.concatenate([before, array, after], axis=dim)
    return array


def efficiency(labels):
    result = jnp.zeros(labels.shape, jnp.float32)
    for label_value in range(4):
        result = result + SURFACE_EFF[label_value] * (labels == label_value).astype(jnp.float32)
    return result


def lateral(extended):
    middle = extended[:, 1:-1]
    padded = jnp.pad(middle, ((0, 0), (0, 0), (1, 1), (1, 1)))
    return (
        extended[:, 2:]
        + extended[:, :-2]
        + padded[:, :, 2:, 1:-1]
        + padded[:, :, :-2, 1:-1]
        + padded[:, :, 1:-1, 2:]
        + padded[:, :, 1:-1, :-2]
        - 6.0 * middle
    )


def shards(
    concentration,
    deposit,
    velocity,
    pore_label,
    diffusivity,
    attach_rate,
    volume,
    conc_cotangent,
    deposit_cotangent,
):
    classes_here = concentration.shape[0]
    coeff_dif = diffusivity[:, None, None, None]
    coeff_rate = attach_rate[:, None, None, None]
    coeff_vol = volume[:, None, None, None]
    collector = efficiency(pore_label)

    def blocking(dep_state):
        partial_sum = jnp.sum(coeff_vol * dep_state, axis=0)
        return jnp.exp(-CLOGGING * lax.psum(partial_sum, "size"))

    def forward_rates(extended, blocked, collect, flow_now):
        middle = extended[:, 1:-1]
        reaction = coeff_rate * collect * blocked * middle
        rate_conc = (
            coeff_dif * lateral(extended) - flow_now * (middle - extended[:, :-2]) - reaction
        )
        return (rate_conc, reaction)

    stacked = jnp.concatenate([concentration, velocity[None]], axis=0)
    first_ext = with_halo(stacked, (("gz", 1),), 1)
    flow_here = first_ext[classes_here, 1:-1]
    flow_above = first_ext[classes_here, 2:]
    blocked_zero = blocking(deposit)
    rate_conc, reaction = forward_rates(
        first_ext[:classes_here], blocked_zero, collector, flow_here
    )
    conc_one = concentration + TIME_STEP * rate_conc
    dep_one = deposit + TIME_STEP * reaction
    blocked_one = blocking(dep_one)
    conc_one_ext = with_halo(conc_one, (("gz", 1),), 1)
    rate_conc, reaction = forward_rates(conc_one_ext, blocked_one, collector, flow_here)
    conc_two = 0.75 * concentration + 0.25 * (conc_one + TIME_STEP * rate_conc)
    dep_two = 0.75 * deposit + 0.25 * (dep_one + TIME_STEP * reaction)
    blocked_two = blocking(dep_two)
    conc_states = (concentration, conc_one, conc_two)
    blocks = (blocked_zero, blocked_one, blocked_two)
    adj_conc = conc_cotangent
    adj_dep = deposit_cotangent
    total_conc = jnp.zeros(concentration.shape, jnp.float32)
    total_dep = jnp.zeros(deposit.shape, jnp.float32)
    for segment_index in (2, 1, 0):
        weight_old, weight_new = MIXING[segment_index]
        push_conc = weight_new * TIME_STEP * adj_conc
        push_ext = with_halo(push_conc, (("gz", 1),), 1)
        uptake = coeff_rate * collector * blocks[segment_index]
        weight = weight_new * TIME_STEP * adj_dep - push_conc
        back_conc = (
            coeff_dif * lateral(push_ext)
            - flow_here * push_conc
            + flow_above * push_ext[:, 2:]
            + uptake * weight
        )
        theta_part = -CLOGGING * jnp.sum(weight * (uptake * conc_states[segment_index]), axis=0)
        theta_grad = lax.psum(theta_part, "size")
        back_conc, back_dep = (back_conc, coeff_vol * theta_grad[None])
        total_conc = total_conc + weight_old * adj_conc
        total_dep = total_dep + weight_old * adj_dep
        adj_conc = weight_new * adj_conc + back_conc
        adj_dep = weight_new * adj_dep + back_dep
    return (total_conc + adj_conc, total_dep + adj_dep)


def solution(mesh):
    in_specs = (
        P("size", "gz", None, None),
        P("size", "gz", None, None),
        P("gz", None, None),
        P("gz", None, None),
        P("size"),
        P("size"),
        P("size"),
        P("size", "gz", None, None),
        P("size", "gz", None, None),
    )
    out_specs = (P("size", "gz", None, None), P("size", "gz", None, None))
    return jax.shard_map(shards, mesh=mesh, in_specs=in_specs, out_specs=out_specs, check_vma=False)
```

profile of v0, /device:TPU:1, one launch (start us, length us, event | category | flops | bytes accessed | tf_op | source)
XLA Modules:
  0.0 333.7 jit_solution(14072504348396859562)
XLA Ops:
  7.2 1.9 multiply_reduce_fusion.4
  9.3 51.8 %all-reduce.12.cloned.1.call-done = f32[4,128,128]{2,1,0:T(8,128)} async-done(((f32[4,128,128]{2,1,0:T(8,128)}), f32[4,128,128]{2,1,0:T(8,128)}) %all-reduce.12.cloned.1.call-update) | async-done | bytes 262160 | tf_op jit(solution)/shard_map/psum | solution.py:65
  64.6 4.0 %collective-permute-start.3 = (f32[3,1,128,128]{3,2,1,0:T(8,128)S(1)}, f32[3,1,128,128]{3,2,1,0:T(8,128)S(1)}, u32[]{:S(2)}, u32[]{:S(2)}) collective-permute-start(f32[3,1,128,128]{3,2,1,0:T(8,128)S(1)} %get-tuple-element.9), channel_id=1, source_target_pairs={{0,1},{1,2},{2,3},{3,4},{4,5},{5,6},{6,7},{7,8},{8,9},{9,10},{10,1... | collective-permute-start | bytes 589832 | tf_op jit(solution)/shard_map/ppermute | solution.py:19
  68.6 42.5 %all-reduce.14.cloned.1.call-done = f32[4,128,128]{2,1,0:T(8,128)} async-done(((f32[4,128,128]{2,1,0:T(8,128)}), f32[4,128,128]{2,1,0:T(8,128)}) %all-reduce.14.cloned.1.call-update) | async-done | bytes 262160 | tf_op jit(solution)/shard_map/psum | solution.py:65
  112.1 1.3 multiply_reduce_fusion.2
  115.5 4.6 %collective-permute-start.7 = (f32[2,1,128,128]{3,2,1,0:T(8,128)}, f32[2,1,128,128]{3,2,1,0:T(8,128)}, u32[]{:S(2)}, u32[]{:S(2)}) collective-permute-start(f32[2,1,128,128]{3,2,1,0:T(8,128)} %get-tuple-element.19), channel_id=1, source_target_pairs={{0,1},{1,2},{2,3},{3,4},{4,5},{5,6},{6,7},{7,8},{8,9},{9,10},{10,1... | collective-permute-start | bytes 393224 | tf_op jit(solution)/shard_map/ppermute | solution.py:19
  120.1 40.9 %all-reduce.16.cloned.1.call-done = f32[4,128,128]{2,1,0:T(8,128)} async-done(((f32[4,128,128]{2,1,0:T(8,128)}), f32[4,128,128]{2,1,0:T(8,128)}) %all-reduce.16.cloned.1.call-update) | async-done | bytes 262160 | tf_op jit(solution)/shard_map/psum | solution.py:65
  162.1 2.4 broadcast_multiply_fusion.2
  166.2 1.3 collective-permute-start
  167.6 4.8 %collective-permute-start.1 = (f32[2,1,128,128]{3,2,1,0:T(8,128)S(1)}, f32[2,1,128,128]{3,2,1,0:T(8,128)}, u32[]{:S(2)}, u32[]{:S(2)}) collective-permute-start(f32[2,1,128,128]{3,2,1,0:T(8,128)S(1)} %get-tuple-element.15), channel_id=1, source_target_pairs={{0,1},{1,2},{2,3},{3,4},{4,5},{5,6},{6,7},{7,8},{8,9},{9,10},{10,1... | collective-permute-start | bytes 393224 | tf_op jit(solution)/shard_map/ppermute | solution.py:19
  174.0 4.2 %collective-permute-done.1 = f32[2,1,128,128]{3,2,1,0:T(8,128)} collective-permute-done((f32[2,1,128,128]{3,2,1,0:T(8,128)S(1)}, f32[2,1,128,128]{3,2,1,0:T(8,128)}, u32[]{:S(2)}, u32[]{:S(2)}) %collective-permute-start.1) | collective-permute-done | bytes 131104 | tf_op jit(solution)/shard_map/ppermute | solution.py:19
  178.2 34.5 %all-reduce.18.cloned.1.call-done = f32[4,128,128]{2,1,0:T(8,128)} async-done(((f32[4,128,128]{2,1,0:T(8,128)}), f32[4,128,128]{2,1,0:T(8,128)}) %all-reduce.18.cloned.1.call-update) | async-done | bytes 262160 | tf_op jit(solution)/shard_map/psum | solution.py:110
  212.8 3.8 %multiply_reduce_fusion.1 = (f32[4,128,128]{2,1,0:T(8,128)S(1)}, f32[2,4,128,128]{3,2,1,0:T(8,128)S(1)}) fusion(f32[2,4,128,128]{3,2,1,0:T(8,128)S(1)} %copy-done.1, f32[2,4,128,128]{3,2,1,0:T(8,128)S(1)} %get-tuple-element.7, f32[4,128,128]{2,1,0:T(8,128)} %all-reduce.18.cloned.1.call-done, f32[4,128,128]{2,1,0:T(8,128)S(1)} %multiply_exponential_fusion.1, ...), kind=kLoop, calls=%fused_computation.110 | loop fusion | flops 3997696 | bytes 4718616 | tf_op jit(solution)/shard_map/reduce_sum | solution.py:109
  218.7 4.6 %collective-permute-start.5 = (f32[2,1,128,128]{3,2,1,0:T(8,128)S(1)}, f32[2,1,128,128]{3,2,1,0:T(8,128)}, u32[]{:S(2)}, u32[]{:S(2)}) collective-permute-start(f32[2,1,128,128]{3,2,1,0:T(8,128)S(1)} %get-tuple-element.13), channel_id=1, source_target_pairs={{0,1},{1,2},{2,3},{3,4},{4,5},{5,6},{6,7},{7,8},{8,9},{9,10},{10,1... | collective-permute-start | bytes 393224 | tf_op jit(solution)/shard_map/ppermute | solution.py:19
  224.3 5.2 %collective-permute-done.5 = f32[2,1,128,128]{3,2,1,0:T(8,128)} collective-permute-done((f32[2,1,128,128]{3,2,1,0:T(8,128)S(1)}, f32[2,1,128,128]{3,2,1,0:T(8,128)}, u32[]{:S(2)}, u32[]{:S(2)}) %collective-permute-start.5) | collective-permute-done | bytes 131104 | tf_op jit(solution)/shard_map/ppermute | solution.py:19
  229.5 34.4 %all-reduce.20.cloned.1.call-done = f32[4,128,128]{2,1,0:T(8,128)} async-done(((f32[4,128,128]{2,1,0:T(8,128)}), f32[4,128,128]{2,1,0:T(8,128)}) %all-reduce.20.cloned.1.call-update) | async-done | bytes 262160 | tf_op jit(solution)/shard_map/psum | solution.py:110
  263.8 3.8 %multiply_reduce_fusion = (f32[4,128,128]{2,1,0:T(8,128)S(1)}, f32[2,4,128,128]{3,2,1,0:T(8,128)S(1)}) fusion(f32[2,4,128,128]{3,2,1,0:T(8,128)S(1)} %copy-done.1, f32[2,4,128,128]{3,2,1,0:T(8,128)S(1)} %copy-done, f32[4,128,128]{2,1,0:T(8,128)} %all-reduce.20.cloned.1.call-done, f32[4,128,128]{2,1,0:T(8,128)} %all-reduce.18.cloned.1.call-done, ...), kind=kLoop, calls=%fused_computation.107 | loop fusion | flops 4521984 | bytes 4980760 | tf_op jit(solution)/shard_map/reduce_sum | solution.py:109
  268.4 1.7 fusion.74
  270.1 1.4 collective-permute-start.8
  271.5 4.6 %collective-permute-start.9 = (f32[2,1,128,128]{3,2,1,0:T(8,128)}, f32[2,1,128,128]{3,2,1,0:T(8,128)}, u32[]{:S(2)}, u32[]{:S(2)}) collective-permute-start(f32[2,1,128,128]{3,2,1,0:T(8,128)} %get-tuple-element.11), channel_id=1, source_target_pairs={{0,1},{1,2},{2,3},{3,4},{4,5},{5,6},{6,7},{7,8},{8,9},{9,10},{10,1... | collective-permute-start | bytes 393224 | tf_op jit(solution)/shard_map/ppermute | solution.py:19
  277.3 4.6 %collective-permute-done.9 = f32[2,1,128,128]{3,2,1,0:T(8,128)} collective-permute-done((f32[2,1,128,128]{3,2,1,0:T(8,128)}, f32[2,1,128,128]{3,2,1,0:T(8,128)}, u32[]{:S(2)}, u32[]{:S(2)}) %collective-permute-start.9) | collective-permute-done | bytes 131104 | tf_op jit(solution)/shard_map/ppermute | solution.py:19
  281.9 4.4 %fusion.14 = f32[2,4,128,128]{3,2,1,0:T(8,128)} fusion(f32[2,4,128,128]{3,2,1,0:T(8,128)S(1)} %get-tuple-element.3, f32[2,4,128,128]{3,2,1,0:T(8,128)} %broadcast_multiply_fusion.1, f32[2,1,128,128]{3,2,1,0:T(8,128)} %collective-permute-done.9, f32[2,1,128,128]{3,2,1,0:T(8,128)S(1)} %collective-permute-done.8, f32[2,4,128,128]{3,2,1,0:T(8,128)S(1)} %get-tuple-element.5, ...), kind=kLoop, calls=%fused_computation.37 | loop fusion | flops 4325376 | bytes 4980760 | tf_op jit(solution)/shard_map/add | solution.py:116
  286.3 38.6 %all-reduce.22.cloned.1.call-done = f32[4,128,128]{2,1,0:T(8,128)} async-done(((f32[4,128,128]{2,1,0:T(8,128)}), f32[4,128,128]{2,1,0:T(8,128)}) %all-reduce.22.cloned.1.call-update) | async-done | bytes 262160 | tf_op jit(solution)/shard_map/psum | solution.py:110
  324.8 2.0 add_add_fusion
  (70 shorter events, 16.0 us)
Async XLA Ops:
  7.2 54.0 %all-reduce.12.cloned.1.call-start = ((), (), s32[]{:S(2)}) async-start(), calls=%async_computation | async-start | bytes 524288 | tf_op jit(solution)/shard_map/psum | solution.py:65
  9.1 53.0 %copy-start.13 = (f32[2]{0:T(128)S(1)}, f32[2]{0:T(128)}, u32[]{:S(2)}) copy-start(f32[2]{0:T(128)} %param.15) | copy-start | bytes 28
  9.1 53.0 %copy-start.14 = (f32[2]{0:T(128)S(1)}, f32[2]{0:T(128)}, u32[]{:S(2)}) copy-start(f32[2]{0:T(128)} %param.14) | copy-start | bytes 28
  9.2 53.0 %copy-start = (f32[2,4,128,128]{3,2,1,0:T(8,128)S(1)}, f32[2,4,128,128]{3,2,1,0:T(8,128)}, u32[]{:S(2)}) copy-start(f32[2,4,128,128]{3,2,1,0:T(8,128)} %param.9) | copy-start | bytes 1572868
  9.2 53.0 %copy-start.3 = (f32[2,4,128,128]{3,2,1,0:T(8,128)S(1)}, f32[2,4,128,128]{3,2,1,0:T(8,128)}, u32[]{:S(2)}) copy-start(f32[2,4,128,128]{3,2,1,0:T(8,128)} %param.10) | copy-start | bytes 1572868
  9.2 101.9 %all-reduce.14.cloned.1.call-start = ((), (), s32[]{:S(2)}) async-start(), calls=%async_computation.1 | async-start | bytes 524288 | tf_op jit(solution)/shard_map/psum | solution.py:65
  63.2 97.9 %all-reduce.16.cloned.1.call-start = ((), (), s32[]{:S(2)}) async-start(), calls=%async_computation.2 | async-start | bytes 524288 | tf_op jit(solution)/shard_map/psum | solution.py:65
  63.2 48.8 %copy-start.15 = (f32[2]{0:T(128)S(1)}, f32[2]{0:T(128)}, u32[]{:S(2)}) copy-start(f32[2]{0:T(128)} %param.13) | copy-start | bytes 28
  63.3 48.8 %collective-permute-start.2 = (f32[3,1,128,128]{3,2,1,0:T(8,128)S(1)}, f32[3,1,128,128]{3,2,1,0:T(8,128)S(1)}, u32[]{:S(2)}, u32[]{:S(2)}) collective-permute-start(f32[3,1,128,128]{3,2,1,0:T(8,128)S(1)} %get-tuple-element.8), channel_id=1, source_target_pairs={{1,0},{2,1},{3,2},{4,3},{5,4},{6,5},{7,6},{8,7},{9,8},{10,9},{11,1... | collective-permute-start | bytes 589832 | tf_op jit(solution)/shard_map/ppermute | solution.py:20
  64.6 47.5 %collective-permute-start.3 = (f32[3,1,128,128]{3,2,1,0:T(8,128)S(1)}, f32[3,1,128,128]{3,2,1,0:T(8,128)S(1)}, u32[]{:S(2)}, u32[]{:S(2)}) collective-permute-start(f32[3,1,128,128]{3,2,1,0:T(8,128)S(1)} %get-tuple-element.9), channel_id=1, source_target_pairs={{0,1},{1,2},{2,3},{3,4},{4,5},{5,6},{6,7},{7,8},{8,9},{9,10},{10,1... | collective-permute-start | bytes 589832 | tf_op jit(solution)/shard_map/ppermute | solution.py:19
  113.4 99.3 %all-reduce.18.cloned.1.call-start = ((), (), s32[]{:S(2)}) async-start(), calls=%async_computation.3 | async-start | bytes 524288 | tf_op jit(solution)/shard_map/psum | solution.py:110
  113.5 48.6 %copy-start.1 = (f32[2,4,128,128]{3,2,1,0:T(8,128)S(1)}, f32[2,4,128,128]{3,2,1,0:T(8,128)}, u32[]{:S(2)}) copy-start(f32[2,4,128,128]{3,2,1,0:T(8,128)} %param.17) | copy-start | bytes 1572868
  113.5 48.6 %copy-start.4 = (f32[2,4,128,128]{3,2,1,0:T(8,128)S(1)}, f32[2,4,128,128]{3,2,1,0:T(8,128)}, u32[]{:S(2)}) copy-start(f32[2,4,128,128]{3,2,1,0:T(8,128)} %param.16) | copy-start | bytes 1572868
  114.2 47.8 %collective-permute-start.6 = (f32[2,1,128,128]{3,2,1,0:T(8,128)}, f32[2,1,128,128]{3,2,1,0:T(8,128)S(1)}, u32[]{:S(2)}, u32[]{:S(2)}) collective-permute-start(f32[2,1,128,128]{3,2,1,0:T(8,128)} %get-tuple-element.18), channel_id=1, source_target_pairs={{1,0},{2,1},{3,2},{4,3},{5,4},{6,5},{7,6},{8,7},{9,8},{10,9},{11,1... | collective-permute-start | bytes 393224 | tf_op jit(solution)/shard_map/ppermute | solution.py:20
  115.5 46.5 %collective-permute-start.7 = (f32[2,1,128,128]{3,2,1,0:T(8,128)}, f32[2,1,128,128]{3,2,1,0:T(8,128)}, u32[]{:S(2)}, u32[]{:S(2)}) collective-permute-start(f32[2,1,128,128]{3,2,1,0:T(8,128)} %get-tuple-element.19), channel_id=1, source_target_pairs={{0,1},{1,2},{2,3},{3,4},{4,5},{5,6},{6,7},{7,8},{8,9},{9,10},{10,1... | collective-permute-start | bytes 393224 | tf_op jit(solution)/shard_map/ppermute | solution.py:19
  165.2 98.6 %all-reduce.20.cloned.1.call-start = ((), (), s32[]{:S(2)}) async-start(), calls=%async_computation.4 | async-start | bytes 524288 | tf_op jit(solution)/shard_map/psum | solution.py:110
  166.2 7.8 %collective-permute-start = (f32[2,1,128,128]{3,2,1,0:T(8,128)S(1)}, f32[2,1,128,128]{3,2,1,0:T(8,128)S(1)}, u32[]{:S(2)}, u32[]{:S(2)}) collective-permute-start(f32[2,1,128,128]{3,2,1,0:T(8,128)S(1)} %get-tuple-element.14), channel_id=1, source_target_pairs={{1,0},{2,1},{3,2},{4,3},{5,4},{6,5},{7,6},{8,7},{9,8},{10,9},{11,1... | collective-permute-start | bytes 393224 | tf_op jit(solution)/shard_map/ppermute | solution.py:20
  167.6 10.7 %collective-permute-start.1 = (f32[2,1,128,128]{3,2,1,0:T(8,128)S(1)}, f32[2,1,128,128]{3,2,1,0:T(8,128)}, u32[]{:S(2)}, u32[]{:S(2)}) collective-permute-start(f32[2,1,128,128]{3,2,1,0:T(8,128)S(1)} %get-tuple-element.15), channel_id=1, source_target_pairs={{0,1},{1,2},{2,3},{3,4},{4,5},{5,6},{6,7},{7,8},{8,9},{9,10},{10,1... | collective-permute-start | bytes 393224 | tf_op jit(solution)/shard_map/ppermute | solution.py:19
  217.3 107.5 %all-reduce.22.cloned.1.call-start = ((), (), s32[]{:S(2)}) async-start(), calls=%async_computation.5 | async-start | bytes 524288 | tf_op jit(solution)/shard_map/psum | solution.py:110
  217.4 46.4 %copy-start.7 = (f32[2,4,128,128]{3,2,1,0:T(8,128)}, f32[2,4,128,128]{3,2,1,0:T(8,128)S(1)}, u32[]{:S(2)}) copy-start(f32[2,4,128,128]{3,2,1,0:T(8,128)S(1)} %broadcast_multiply_fusion) | copy-start | bytes 1572868
  217.4 6.8 %collective-permute-start.4 = (f32[2,1,128,128]{3,2,1,0:T(8,128)S(1)}, f32[2,1,128,128]{3,2,1,0:T(8,128)S(1)}, u32[]{:S(2)}, u32[]{:S(2)}) collective-permute-start(f32[2,1,128,128]{3,2,1,0:T(8,128)S(1)} %get-tuple-element.12), channel_id=1, source_target_pairs={{1,0},{2,1},{3,2},{4,3},{5,4},{6,5},{7,6},{8,7},{9,8},{10,9},{11,1... | collective-permute-start | bytes 393224 | tf_op jit(solution)/shard_map/ppermute | solution.py:20
  218.7 10.7 %collective-permute-start.5 = (f32[2,1,128,128]{3,2,1,0:T(8,128)S(1)}, f32[2,1,128,128]{3,2,1,0:T(8,128)}, u32[]{:S(2)}, u32[]{:S(2)}) collective-permute-start(f32[2,1,128,128]{3,2,1,0:T(8,128)S(1)} %get-tuple-element.13), channel_id=1, source_target_pairs={{0,1},{1,2},{2,3},{3,4},{4,5},{5,6},{6,7},{7,8},{8,9},{9,10},{10,1... | collective-permute-start | bytes 393224 | tf_op jit(solution)/shard_map/ppermute | solution.py:19
  270.1 7.2 %collective-permute-start.8 = (f32[2,1,128,128]{3,2,1,0:T(8,128)}, f32[2,1,128,128]{3,2,1,0:T(8,128)S(1)}, u32[]{:S(2)}, u32[]{:S(2)}) collective-permute-start(f32[2,1,128,128]{3,2,1,0:T(8,128)} %get-tuple-element.10), channel_id=1, source_target_pairs={{1,0},{2,1},{3,2},{4,3},{5,4},{6,5},{7,6},{8,7},{9,8},{10,9},{11,1... | collective-permute-start | bytes 393224 | tf_op jit(solution)/shard_map/ppermute | solution.py:20
  271.5 10.3 %collective-permute-start.9 = (f32[2,1,128,128]{3,2,1,0:T(8,128)}, f32[2,1,128,128]{3,2,1,0:T(8,128)}, u32[]{:S(2)}, u32[]{:S(2)}) collective-permute-start(f32[2,1,128,128]{3,2,1,0:T(8,128)} %get-tuple-element.11), channel_id=1, source_target_pairs={{0,1},{1,2},{2,3},{3,4},{4,5},{5,6},{6,7},{7,8},{8,9},{9,10},{10,1... | collective-permute-start | bytes 393224 | tf_op jit(solution)/shard_map/ppermute | solution.py:19
  (8 other events, 47.8 us)
Sparse Core Ops, SparseCore 0:
  11.2 49.9 all-reduce.11
  64.6 46.4 all-reduce.13
  114.2 46.7 all-reduce.15
  165.3 47.3 all-reduce.17
  217.4 46.3 all-reduce.19
  277.0 47.7 all-reduce.21
where the time goes:
time: 334 us
  waiting for transfers between devices  258 us (77%)
  starting transfers between devices  29.5 us (9%)
  other arithmetic  28.3 us (8%)
  between operations  14.4 us (4%)
  local copies, waits for them, and re-layouts  3.47 us (1%)
    psum x3, waiting for transfers between devices, blocking(): return jnp.exp(-CLOGGING * lax.psum(partial_sum, 'size'))  135 us
    psum x3, waiting for transfers between devices, shards(): theta_grad = lax.psum(theta_part, 'size')  107 us
    ppermute x5, starting transfers between devices, with_halo(): before = lax.ppermute(last, axis, up)  22.7 us
    ppermute x5, waiting for transfers between devices, with_halo(): before = lax.ppermute(last, axis, up)  14 us
    reduce_sum x2, other arithmetic, shards(): jnp.sum(weight * (uptake * conc_states[segment_index]), axis=0)  7.57 us
  transfers between devices with their start and end apart: 16, of which 11 were waited for; matrix products, arithmetic and copies ran while one was open for 3% of the time, Pallas kernels for 0%

commit v1 on v0

--- a/solution.py
+++ b/solution.py
@@ -107,7 +107,8 @@
             + uptake * weight
         )
         theta_part = -CLOGGING * jnp.sum(weight * (uptake * conc_states[segment_index]), axis=0)
-        theta_grad = lax.psum(theta_part, "size")
+        parts = lax.all_gather(theta_part, "size", axis=0, tiled=False)
+        theta_grad = parts.sum(axis=0)
         back_conc, back_dep = (back_conc, coeff_vol * theta_grad[None])
         total_conc = total_conc + weight_old * adj_conc
         total_dep = total_dep + weight_old * adj_dep

time: 334 us -> 257 us (0.77)
  waiting for transfers between devices: 258 us -> 183 us
    psum x3 -> x0, waiting for transfers between devices: 107 us -> none  [shards(): theta_grad = lax.psum(theta_part, 'size')]
    all_gather x0 -> x3, waiting for transfers between devices: none -> 42 us  [shards(): parts = lax.all_gather(theta_part, 'size', axis=0, tiled=False)]
    ppermute x5, waiting for transfers between devices: 14 us -> 4.59 us  [with_halo(): before = lax.ppermute(last, axis, up)]
    reduce_sum x0 -> x3, other arithmetic: none -> 4.62 us  [shards(): theta_grad = parts.sum(axis=0)]
    add x2, other arithmetic: 6.45 us -> 2.58 us  [shards(): return (total_conc + adj_conc, total_dep + adj_dep)]
  transfers between devices with their start and end apart: 16 -> 16, of which waited for: 11 -> 8; matrix products, arithmetic and copies ran while one was open for 3% -> 4% of each run, Pallas kernels for 0% -> 0%
where the time goes in v1:
time: 257 us
  waiting for transfers between devices  183 us (71%)
  starting transfers between devices  28.1 us (11%)
  other arithmetic  26.7 us (10%)
  between operations  14.5 us (6%)
  local copies, waits for them, and re-layouts  3.89 us (2%)
    psum x3, waiting for transfers between devices, blocking(): return jnp.exp(-CLOGGING * lax.psum(partial_sum, 'size'))  135 us
    all_gather x3, waiting for transfers between devices, shards(): parts = lax.all_gather(theta_part, 'size', axis=0, tiled=False)  42 us
    ppermute x5, starting transfers between devices, with_halo(): before = lax.ppermute(last, axis, up)  21.3 us
    reduce_sum x2, other arithmetic, shards(): jnp.sum(weight * (uptake * conc_states[segment_index]), axis=0)  6.61 us
    ppermute x5, starting transfers between devices, with_halo(): after = lax.ppermute(initial, axis, down)  6.56 us
  transfers between devices with their start and end apart: 16, of which 8 were waited for; matrix products, arithmetic and copies ran while one was open for 4% of the time, Pallas kernels for 0%

profile of v1, /device:TPU:1, one launch (start us, length us, event | category | flops | bytes accessed | tf_op | source)
XLA Modules:
  0.0 256.6 jit_solution(6503182846273364786)
XLA Ops:
  7.3 2.0 multiply_reduce_fusion.4
  9.4 51.8 %all-reduce.9.cloned.1.call-done = f32[4,128,128]{2,1,0:T(8,128)} async-done(((f32[4,128,128]{2,1,0:T(8,128)}), f32[4,128,128]{2,1,0:T(8,128)}) %all-reduce.9.cloned.1.call-update) | async-done | bytes 262160 | tf_op jit(solution)/shard_map/psum | solution.py:65
  64.6 4.0 %collective-permute-start.3 = (f32[3,1,128,128]{3,2,1,0:T(8,128)S(1)}, f32[3,1,128,128]{3,2,1,0:T(8,128)S(1)}, u32[]{:S(2)}, u32[]{:S(2)}) collective-permute-start(f32[3,1,128,128]{3,2,1,0:T(8,128)S(1)} %get-tuple-element.9), channel_id=1, source_target_pairs={{0,1},{1,2},{2,3},{3,4},{4,5},{5,6},{6,7},{7,8},{8,9},{9,10},{10,1... | collective-permute-start | bytes 589832 | tf_op jit(solution)/shard_map/ppermute | solution.py:19
  68.6 42.7 %all-reduce.11.cloned.1.call-done = f32[4,128,128]{2,1,0:T(8,128)} async-done(((f32[4,128,128]{2,1,0:T(8,128)}), f32[4,128,128]{2,1,0:T(8,128)}) %all-reduce.11.cloned.1.call-update) | async-done | bytes 262160 | tf_op jit(solution)/shard_map/psum | solution.py:65
  112.3 1.3 multiply_reduce_fusion.2
  115.8 4.6 %collective-permute-start.7 = (f32[2,1,128,128]{3,2,1,0:T(8,128)}, f32[2,1,128,128]{3,2,1,0:T(8,128)}, u32[]{:S(2)}, u32[]{:S(2)}) collective-permute-start(f32[2,1,128,128]{3,2,1,0:T(8,128)} %get-tuple-element.19), channel_id=1, source_target_pairs={{0,1},{1,2},{2,3},{3,4},{4,5},{5,6},{6,7},{7,8},{8,9},{9,10},{10,1... | collective-permute-start | bytes 393224 | tf_op jit(solution)/shard_map/ppermute | solution.py:19
  120.4 40.9 %all-reduce.13.cloned.1.call-done = f32[4,128,128]{2,1,0:T(8,128)} async-done(((f32[4,128,128]{2,1,0:T(8,128)}), f32[4,128,128]{2,1,0:T(8,128)}) %all-reduce.13.cloned.1.call-update) | async-done | bytes 262160 | tf_op jit(solution)/shard_map/psum | solution.py:65
  162.3 2.4 broadcast_multiply_fusion.2
  165.5 1.7 fusion.76
  168.4 4.0 %collective-permute-start.1 = (f32[2,1,128,128]{3,2,1,0:T(8,128)S(1)}, f32[2,1,128,128]{3,2,1,0:T(8,128)S(1)}, u32[]{:S(2)}, u32[]{:S(2)}) collective-permute-start(f32[2,1,128,128]{3,2,1,0:T(8,128)S(1)} %get-tuple-element.15), channel_id=1, source_target_pairs={{0,1},{1,2},{2,3},{3,4},{4,5},{5,6},{6,7},{7,8},{8,9},{9,10},{10,1... | collective-permute-start | bytes 393224 | tf_op jit(solution)/shard_map/ppermute | solution.py:19
  173.4 14.9 %all-gather.7.cloned.1.call-done = f32[16,128,128]{2,1,0:T(8,128)} async-done(((f32[4,128,128]{2,1,0:T(8,128)}), f32[16,128,128]{2,1,0:T(8,128)}) %all-gather.7.cloned.1.call-update) | async-done | bytes 1048592 | tf_op jit(solution)/shard_map/all_gather | solution.py:110
  188.3 1.3 reduce_sum.85
  190.3 3.4 %multiply_reduce_fusion.1 = (f32[4,128,128]{2,1,0:T(8,128)S(1)}, f32[2,4,128,128]{3,2,1,0:T(8,128)S(1)}) fusion(f32[2,4,128,128]{3,2,1,0:T(8,128)S(1)} %copy-done.1, f32[2,4,128,128]{3,2,1,0:T(8,128)S(1)} %get-tuple-element.7, f32[4,128,128]{2,1,0:T(8,128)S(1)} %reduce_sum.85, f32[4,128,128]{2,1,0:T(8,128)S(1)} %multiply_exponential_fusion.1, ...), kind=kLoop, calls=%fused_computation.110 | loop fusion | flops 3997696 | bytes 4718616 | tf_op jit(solution)/shard_map/reduce_sum | solution.py:109
  196.6 4.6 %collective-permute-start.5 = (f32[2,1,128,128]{3,2,1,0:T(8,128)}, f32[2,1,128,128]{3,2,1,0:T(8,128)}, u32[]{:S(2)}, u32[]{:S(2)}) collective-permute-start(f32[2,1,128,128]{3,2,1,0:T(8,128)} %get-tuple-element.13), channel_id=1, source_target_pairs={{0,1},{1,2},{2,3},{3,4},{4,5},{5,6},{6,7},{7,8},{8,9},{9,10},{10,1... | collective-permute-start | bytes 393224 | tf_op jit(solution)/shard_map/ppermute | solution.py:19
  201.2 17.2 %all-gather.9.cloned.1.call-done = f32[16,128,128]{2,1,0:T(8,128)} async-done(((f32[4,128,128]{2,1,0:T(8,128)}), f32[16,128,128]{2,1,0:T(8,128)}) %all-gather.9.cloned.1.call-update) | async-done | bytes 1048592 | tf_op jit(solution)/shard_map/all_gather | solution.py:110
  218.4 2.0 reduce_sum.87
  220.4 3.2 %multiply_reduce_fusion = (f32[4,128,128]{2,1,0:T(8,128)S(1)}, f32[2,4,128,128]{3,2,1,0:T(8,128)S(1)}) fusion(f32[2,4,128,128]{3,2,1,0:T(8,128)S(1)} %copy-done.1, f32[2,4,128,128]{3,2,1,0:T(8,128)S(1)} %copy-done, f32[4,128,128]{2,1,0:T(8,128)} %reduce_sum.87, f32[4,128,128]{2,1,0:T(8,128)S(1)} %reduce_sum.85, ...), kind=kLoop, calls=%fused_computation.107 | loop fusion | flops 4521984 | bytes 4980760 | tf_op jit(solution)/shard_map/reduce_sum | solution.py:109
  224.5 1.4 collective-permute-start.8
  225.9 4.0 %collective-permute-start.9 = (f32[2,1,128,128]{3,2,1,0:T(8,128)S(1)}, f32[2,1,128,128]{3,2,1,0:T(8,128)S(1)}, u32[]{:S(2)}, u32[]{:S(2)}) collective-permute-start(f32[2,1,128,128]{3,2,1,0:T(8,128)S(1)} %get-tuple-element.11), channel_id=1, source_target_pairs={{0,1},{1,2},{2,3},{3,4},{4,5},{5,6},{6,7},{7,8},{8,9},{9,10},{10,1... | collective-permute-start | bytes 393224 | tf_op jit(solution)/shard_map/ppermute | solution.py:19
  229.9 1.4 collective-permute-done.8
  231.3 4.6 %collective-permute-done.9 = f32[2,1,128,128]{3,2,1,0:T(8,128)S(1)} collective-permute-done((f32[2,1,128,128]{3,2,1,0:T(8,128)S(1)}, f32[2,1,128,128]{3,2,1,0:T(8,128)S(1)}, u32[]{:S(2)}, u32[]{:S(2)}) %collective-permute-start.9) | collective-permute-done | bytes 131104 | tf_op jit(solution)/shard_map/ppermute | solution.py:19
  235.9 1.5 fusion.14
  237.4 10.0 %all-gather.11.cloned.1.call-done = f32[16,128,128]{2,1,0:T(8,128)} async-done(((f32[4,128,128]{2,1,0:T(8,128)}), f32[16,128,128]{2,1,0:T(8,128)}) %all-gather.11.cloned.1.call-update) | async-done | bytes 1048592 | tf_op jit(solution)/shard_map/all_gather | solution.py:110
  247.3 1.3 reduce_sum.89
  (75 shorter events, 16.1 us)
Async XLA Ops:
  7.2 55.0 %copy-start.14 = (f32[2]{0:T(128)S(1)}, f32[2]{0:T(128)}, u32[]{:S(2)}) copy-start(f32[2]{0:T(128)} %param.15) | copy-start | bytes 28
  7.2 55.0 %copy-start.3 = (f32[2,4,128,128]{3,2,1,0:T(8,128)S(1)}, f32[2,4,128,128]{3,2,1,0:T(8,128)}, u32[]{:S(2)}) copy-start(f32[2,4,128,128]{3,2,1,0:T(8,128)} %param.10) | copy-start | bytes 1572868
  7.2 55.0 %copy-start.15 = (f32[2]{0:T(128)S(1)}, f32[2]{0:T(128)}, u32[]{:S(2)}) copy-start(f32[2]{0:T(128)} %param.14) | copy-start | bytes 28
  7.2 55.0 %copy-start = (f32[2,4,128,128]{3,2,1,0:T(8,128)S(1)}, f32[2,4,128,128]{3,2,1,0:T(8,128)}, u32[]{:S(2)}) copy-start(f32[2,4,128,128]{3,2,1,0:T(8,128)} %param.9) | copy-start | bytes 1572868
  7.2 54.0 %all-reduce.9.cloned.1.call-start = ((), (), s32[]{:S(2)}) async-start(), calls=%async_computation | async-start | bytes 524288 | tf_op jit(solution)/shard_map/psum | solution.py:65
  9.2 102.1 %all-reduce.11.cloned.1.call-start = ((), (), s32[]{:S(2)}) async-start(), calls=%async_computation.1 | async-start | bytes 524288 | tf_op jit(solution)/shard_map/psum | solution.py:65
  63.2 49.2 %copy-start.16 = (f32[2]{0:T(128)S(1)}, f32[2]{0:T(128)}, u32[]{:S(2)}) copy-start(f32[2]{0:T(128)} %param.13) | copy-start | bytes 28
  63.2 98.1 %all-reduce.13.cloned.1.call-start = ((), (), s32[]{:S(2)}) async-start(), calls=%async_computation.2 | async-start | bytes 524288 | tf_op jit(solution)/shard_map/psum | solution.py:65
  63.3 49.0 %collective-permute-start.2 = (f32[3,1,128,128]{3,2,1,0:T(8,128)S(1)}, f32[3,1,128,128]{3,2,1,0:T(8,128)S(1)}, u32[]{:S(2)}, u32[]{:S(2)}) collective-permute-start(f32[3,1,128,128]{3,2,1,0:T(8,128)S(1)} %get-tuple-element.8), channel_id=1, source_target_pairs={{1,0},{2,1},{3,2},{4,3},{5,4},{6,5},{7,6},{8,7},{9,8},{10,9},{11,1... | collective-permute-start | bytes 589832 | tf_op jit(solution)/shard_map/ppermute | solution.py:20
  64.6 47.7 %collective-permute-start.3 = (f32[3,1,128,128]{3,2,1,0:T(8,128)S(1)}, f32[3,1,128,128]{3,2,1,0:T(8,128)S(1)}, u32[]{:S(2)}, u32[]{:S(2)}) collective-permute-start(f32[3,1,128,128]{3,2,1,0:T(8,128)S(1)} %get-tuple-element.9), channel_id=1, source_target_pairs={{0,1},{1,2},{2,3},{3,4},{4,5},{5,6},{6,7},{7,8},{8,9},{9,10},{10,1... | collective-permute-start | bytes 589832 | tf_op jit(solution)/shard_map/ppermute | solution.py:19
  113.7 48.6 %copy-start.1 = (f32[2,4,128,128]{3,2,1,0:T(8,128)S(1)}, f32[2,4,128,128]{3,2,1,0:T(8,128)}, u32[]{:S(2)}) copy-start(f32[2,4,128,128]{3,2,1,0:T(8,128)} %param.17) | copy-start | bytes 1572868
  113.7 48.6 %copy-start.4 = (f32[2,4,128,128]{3,2,1,0:T(8,128)S(1)}, f32[2,4,128,128]{3,2,1,0:T(8,128)}, u32[]{:S(2)}) copy-start(f32[2,4,128,128]{3,2,1,0:T(8,128)} %param.16) | copy-start | bytes 1572868
  113.7 74.6 %all-gather.7.cloned.1.call-start = ((), (), s32[]{:S(2)}) async-start(), calls=%async_computation.3 | async-start | bytes 1310720 | tf_op jit(solution)/shard_map/all_gather | solution.py:110
  114.5 47.8 %collective-permute-start.6 = (f32[2,1,128,128]{3,2,1,0:T(8,128)}, f32[2,1,128,128]{3,2,1,0:T(8,128)S(1)}, u32[]{:S(2)}, u32[]{:S(2)}) collective-permute-start(f32[2,1,128,128]{3,2,1,0:T(8,128)} %get-tuple-element.18), channel_id=1, source_target_pairs={{1,0},{2,1},{3,2},{4,3},{5,4},{6,5},{7,6},{8,7},{9,8},{10,9},{11,1... | collective-permute-start | bytes 393224 | tf_op jit(solution)/shard_map/ppermute | solution.py:20
  115.8 46.5 %collective-permute-start.7 = (f32[2,1,128,128]{3,2,1,0:T(8,128)}, f32[2,1,128,128]{3,2,1,0:T(8,128)}, u32[]{:S(2)}, u32[]{:S(2)}) collective-permute-start(f32[2,1,128,128]{3,2,1,0:T(8,128)} %get-tuple-element.19), channel_id=1, source_target_pairs={{0,1},{1,2},{2,3},{3,4},{4,5},{5,6},{6,7},{7,8},{8,9},{9,10},{10,1... | collective-permute-start | bytes 393224 | tf_op jit(solution)/shard_map/ppermute | solution.py:19
  165.4 53.0 %all-gather.9.cloned.1.call-start = ((), (), s32[]{:S(2)}) async-start(), calls=%async_computation.4 | async-start | bytes 1310720 | tf_op jit(solution)/shard_map/all_gather | solution.py:110
  167.1 22.5 %collective-permute-start = (f32[2,1,128,128]{3,2,1,0:T(8,128)}, f32[2,1,128,128]{3,2,1,0:T(8,128)S(1)}, u32[]{:S(2)}, u32[]{:S(2)}) collective-permute-start(f32[2,1,128,128]{3,2,1,0:T(8,128)} %get-tuple-element.14), channel_id=1, source_target_pairs={{1,0},{2,1},{3,2},{4,3},{5,4},{6,5},{7,6},{8,7},{9,8},{10,9},{11,1... | collective-permute-start | bytes 393224 | tf_op jit(solution)/shard_map/ppermute | solution.py:20
  168.4 21.2 %collective-permute-start.1 = (f32[2,1,128,128]{3,2,1,0:T(8,128)S(1)}, f32[2,1,128,128]{3,2,1,0:T(8,128)S(1)}, u32[]{:S(2)}, u32[]{:S(2)}) collective-permute-start(f32[2,1,128,128]{3,2,1,0:T(8,128)S(1)} %get-tuple-element.15), channel_id=1, source_target_pairs={{0,1},{1,2},{2,3},{3,4},{4,5},{5,6},{6,7},{7,8},{8,9},{9,10},{10,1... | collective-permute-start | bytes 393224 | tf_op jit(solution)/shard_map/ppermute | solution.py:19
  194.4 52.9 %all-gather.11.cloned.1.call-start = ((), (), s32[]{:S(2)}) async-start(), calls=%async_computation.5 | async-start | bytes 1310720 | tf_op jit(solution)/shard_map/all_gather | solution.py:110
  194.5 25.9 %copy-start.7 = (f32[2,4,128,128]{3,2,1,0:T(8,128)}, f32[2,4,128,128]{3,2,1,0:T(8,128)S(1)}, u32[]{:S(2)}) copy-start(f32[2,4,128,128]{3,2,1,0:T(8,128)S(1)} %broadcast_multiply_fusion) | copy-start | bytes 1572868
  195.3 25.1 %collective-permute-start.4 = (f32[2,1,128,128]{3,2,1,0:T(8,128)}, f32[2,1,128,128]{3,2,1,0:T(8,128)S(1)}, u32[]{:S(2)}, u32[]{:S(2)}) collective-permute-start(f32[2,1,128,128]{3,2,1,0:T(8,128)} %get-tuple-element.12), channel_id=1, source_target_pairs={{1,0},{2,1},{3,2},{4,3},{5,4},{6,5},{7,6},{8,7},{9,8},{10,9},{11,1... | collective-permute-start | bytes 393224 | tf_op jit(solution)/shard_map/ppermute | solution.py:20
  196.6 23.8 %collective-permute-start.5 = (f32[2,1,128,128]{3,2,1,0:T(8,128)}, f32[2,1,128,128]{3,2,1,0:T(8,128)}, u32[]{:S(2)}, u32[]{:S(2)}) collective-permute-start(f32[2,1,128,128]{3,2,1,0:T(8,128)} %get-tuple-element.13), channel_id=1, source_target_pairs={{0,1},{1,2},{2,3},{3,4},{4,5},{5,6},{6,7},{7,8},{8,9},{9,10},{10,1... | collective-permute-start | bytes 393224 | tf_op jit(solution)/shard_map/ppermute | solution.py:19
  224.5 6.8 %collective-permute-start.8 = (f32[2,1,128,128]{3,2,1,0:T(8,128)S(1)}, f32[2,1,128,128]{3,2,1,0:T(8,128)S(1)}, u32[]{:S(2)}, u32[]{:S(2)}) collective-permute-start(f32[2,1,128,128]{3,2,1,0:T(8,128)S(1)} %get-tuple-element.10), channel_id=1, source_target_pairs={{1,0},{2,1},{3,2},{4,3},{5,4},{6,5},{7,6},{8,7},{9,8},{10,9},{11,1... | collective-permute-start | bytes 393224 | tf_op jit(solution)/shard_map/ppermute | solution.py:20
  225.9 10.0 %collective-permute-start.9 = (f32[2,1,128,128]{3,2,1,0:T(8,128)S(1)}, f32[2,1,128,128]{3,2,1,0:T(8,128)S(1)}, u32[]{:S(2)}, u32[]{:S(2)}) collective-permute-start(f32[2,1,128,128]{3,2,1,0:T(8,128)S(1)} %get-tuple-element.11), channel_id=1, source_target_pairs={{0,1},{1,2},{2,3},{3,4},{4,5},{5,6},{6,7},{7,8},{8,9},{9,10},{10,1... | collective-permute-start | bytes 393224 | tf_op jit(solution)/shard_map/ppermute | solution.py:19
  (9 other events, 50.1 us)
Sparse Core Ops, SparseCore 0:
  11.3 49.9 all-reduce.8
  64.6 46.6 all-reduce.10
  114.5 46.7 all-reduce.12
  165.6 22.6 all-gather.6
  194.5 23.8 all-gather.8
  224.5 22.7 all-gather.10
